TPU v7x, 256 devices: a whole 4x4x8 slice. The times are simulated.
256 devices in a mesh: snode: 64 (over z, x, core), panel: 4 (over y).
Axes of the slice: x: 4, y: 4, z: 8, core: 2. Of those that a mesh axis runs over, the one named last changes fastest.
Arguments:
- top_inverse: float32 [1280, 1280], P('panel')
- diag_inverse: float32 [3, 64, 512, 512], P(None, 'snode', 'panel')
- u_factor: float32 [3, 64, 768, 512], P(None, 'snode'), may hold values from -0.21875 to 0.21875
- parent_map: int32 [2, 64], replicated, may hold values from 0 to 63, as said below
- lengths: int32 [3, 64], replicated, may hold values from 192 to 768, as said below
- rows_map: int32 [3, 64, 768], replicated, may hold values from 0 to 1279, as said below
Outputs:
- diag_block: float32 [3, 64, 512, 512], P(None, 'snode', 'panel')
- off_block: float32 [3, 64, 768, 512], P(None, 'snode', 'panel')
Inputs may be any that keep to these rules, and one draw needn't show every extreme that they name: `parent_map`: supernode n of a level is held on snode device n. The parent of a supernode of level l + 1 is held on the same device or on the one before it along snode, the last device standing before the first. `lengths`: every level has a supernode with exactly 768 live structure rows. `top_inverse` and every `diag_inverse[l, n]` are symmetric (each is the inverse of a symmetric positive definite matrix), so every full_block is symmetric. For a below lengths[l, n], the entries rows_map[l, n, a] are distinct and lie below 512 plus the parent's length (1280 at level 0); entries from the length on are 0.
All inputs are finite; a program needn't handle non-finite values.
Results may differ from a plain program's by a relative error of at most 0.0003.
Values sent between devices are 32-bit elements; how exact they have to be, the bound alone decides.
A program may use at most 128 MiB of HBM per device.

v0:
```python
import jax
import jax.numpy as jnp
from jax import lax
from jax.sharding import PartitionSpec as P

HIGHEST = lax.Precision.HIGHEST


def from_behind(value, axis, steps):
    count = lax.axis_size(axis)
    pairs = [(source, (source + steps) % count) for source in range(count)]
    return lax.ppermute(value, axis, pairs)


def extract_block(parent_block, row_index, live_rows):
    row_total = row_index.shape[0]
    live_mask = (jnp.arange(row_total, dtype=jnp.int32) < live_rows).astype(jnp.float32)
    picked = jnp.take(jnp.take(parent_block, row_index, axis=0), row_index, axis=1)
    return picked * live_mask[:, None] * live_mask[None, :]


def assemble(diag_part, off_part, inner_part):
    upper_rows = jnp.concatenate([diag_part, off_part.T], axis=1)
    lower_rows = jnp.concatenate([off_part, inner_part], axis=1)
    return jnp.concatenate([upper_rows, lower_rows], axis=0)


def local(top_inverse, diag_inverse, u_factor, parent_map, lengths, rows_map):
    tier_count = u_factor.shape[0]
    slot_count = u_factor.shape[1]
    struct_rows = u_factor.shape[2]
    col_width = u_factor.shape[3]
    panels = lax.axis_size("panel")
    owner_index = lax.axis_index("snode")
    panel_index = lax.axis_index("panel")
    row_share = struct_rows // panels
    narrow = col_width // panels
    top_full = lax.all_gather(top_inverse, "panel", axis=0, tiled=True)
    diag_tiers = []
    off_tiers = []
    blocks_prev = []
    for tier_index in range(tier_count):
        inner_list = []
        if tier_index == 0:
            slot_index = 0
            flat_index = owner_index * slot_count + slot_index
            inner_list.append(
                extract_block(top_full, rows_map[0, flat_index], lengths[0, flat_index])
            )
        else:
            stacked = jnp.stack(blocks_prev)
            arrived = from_behind(stacked, "snode", 1)
            slot_index = 0
            flat_index = owner_index * slot_count + slot_index
            parent = parent_map[tier_index - 1, flat_index]
            chosen = jnp.where(
                parent // slot_count == owner_index,
                stacked[parent % slot_count],
                arrived[parent % slot_count],
            )
            inner_list.append(
                extract_block(
                    chosen, rows_map[tier_index, flat_index], lengths[tier_index, flat_index]
                )
            )
        blocks_next = []
        slot_index = 0
        inner_block = inner_list[slot_index]
        u_block = u_factor[tier_index, slot_index]
        inner_rows = lax.dynamic_slice_in_dim(inner_block, panel_index * row_share, row_share, 0)
        off_rows = -jnp.dot(inner_rows, u_block, precision=HIGHEST)
        u_rows = lax.dynamic_slice_in_dim(u_block, panel_index * row_share, row_share, 0)

        def partial_term(row_start, row_count, u_rows=u_rows, off_rows=off_rows):
            return jnp.dot(u_rows.T, off_rows, precision=HIGHEST)

        diag_rows = diag_inverse[tier_index, slot_index] - lax.psum_scatter(
            partial_term(jnp.int32(0), lax.axis_size("panel") * narrow),
            "panel",
            scatter_dimension=0,
            tiled=True,
        )
        if tier_index + 1 < tier_count:
            diag_full, off_full = (
                lax.all_gather(diag_rows, "panel", axis=0, tiled=True),
                lax.all_gather(off_rows, "panel", axis=0, tiled=True),
            )
        if tier_index + 1 < tier_count:
            blocks_next.append(assemble(diag_full, off_full, inner_block))
        tier_diag = [diag_rows]
        tier_off = [off_rows]
        diag_tiers.append(jnp.stack(tier_diag))
        off_tiers.append(jnp.stack(tier_off))
        blocks_prev = blocks_next
    return (jnp.stack(diag_tiers), jnp.stack(off_tiers))


def solution(mesh):
    return jax.shard_map(
        local,
        mesh=mesh,
        in_specs=(
            P("panel", None),
            P(None, "snode", "panel", None),
            P(None, "snode", None, None),
            P(),
            P(),
            P(),
        ),
        out_specs=(P(None, "snode", "panel", None), P(None, "snode", "panel", None)),
        check_vma=False,
    )
```

profile of v0, /device:TPU:16, one launch (start us, length us, event | category | flops | bytes accessed | tf_op | source)
XLA Modules:
  0.0 582.2 jit_solution(4603471194339071730)
XLA Ops:
  7.2 0.7 all-gather.6.cloned.1.call-update
  8.0 1.5 constant_dynamic-slice_fusion.2
  9.4 0.8 dynamic-slice_reduce_fusion
  10.3 0.7 fusion.35
  10.9 4.6 fusion.47
  15.5 67.0 %all-gather.6.cloned.1.call-done = f32[1280,1280]{1,0:T(8,128)} async-done(((f32[320,1280]{1,0:T(8,128)}), f32[1280,1280]{1,0:T(8,128)}) %all-gather.6.cloned.1.call-update) | async-done | bytes 6553616 | tf_op jit(solution)/shard_map/all_gather | solution.py:38
  82.5 8.2 %gather_fusion = f32[768,1280]{1,0:T(8,128)} fusion(f32[1280,1280]{1,0:T(8,128)} %all-gather.6.cloned.1.call-done, s32[1024]{0:T(1024)S(1)} %pad_clamp_fusion.2), kind=kCustom, calls=%fused_computation.clone | custom fusion | bytes 7867392 | tf_op jit(solution)/shard_map/jit(_take)/gather | solution.py:18
  90.6 4.4 broadcast_select_fusion.2
  95.1 5.5 copy.9
  100.6 6.2 %gather_fusion.1 = f32[768,768]{1,0:T(8,128)} fusion(f32[768,1280]{0,1:T(8,128)} %copy.9, s32[1024]{0:T(1024)S(1)} %pad_clamp_fusion.2), kind=kCustom, calls=%fused_computation.1.clone | custom fusion | bytes 4721664 | tf_op jit(solution)/shard_map/jit(_take)/gather | solution.py:18
  106.8 2.0 fusion.3
  108.8 3.3 fusion.10
  112.1 3.2 fusion.29
  115.4 0.0 all-gather.10.cloned.1.call-start
  115.4 0.7 all-gather.10.cloned.1.call-update
  116.1 0.0 all-gather.8.cloned.1.call-start
  116.1 2.0 fusion.48
  118.1 0.1 copy.25
  118.2 23.1 %reduce-scatter.4.cloned.1.call-done = f32[128,512]{0,1:T(8,128)} async-done(((f32[512,512]{0,1:T(8,128)}), f32[128,512]{0,1:T(8,128)}) %reduce-scatter.4.cloned.1.call-update) | async-done | bytes 262160 | tf_op jit(solution)/shard_map/reduce_scatter | solution.py:77
  141.4 1.7 bitcast_subtract_fusion.2
  143.1 0.0 reduce-scatter.6.cloned.1.call-start
  143.1 30.0 %all-gather.10.cloned.1.call-done = f32[768,512]{1,0:T(8,128)} async-done(((f32[192,512]{1,0:T(8,128)}), f32[768,512]{1,0:T(8,128)}) %all-gather.10.cloned.1.call-update) | async-done | bytes 1572880 | tf_op jit(solution)/shard_map/all_gather | solution.py:86
  173.1 3.0 copy.12
  176.1 28.2 %all-gather.8.cloned.1.call-done = f32[512,512]{0,1:T(8,128)} async-done(((f32[128,512]{0,1:T(8,128)}), f32[512,512]{0,1:T(8,128)}) %all-gather.8.cloned.1.call-update) | async-done | bytes 1048592 | tf_op jit(solution)/shard_map/all_gather | solution.py:85
  204.3 5.5 fusion.1
  210.6 0.5 fusion.36
  211.1 75.6 %collective-permute-done = f32[1,1280,1280]{1,2,0:T(8,128)} collective-permute-done((f32[1,1280,1280]{1,2,0:T(8,128)}, f32[1,1280,1280]{1,2,0:T(8,128)}, u32[]{:S(2)}, u32[]{:S(2)}) %collective-permute-start) | collective-permute-done | bytes 6553632 | tf_op jit(solution)/shard_map/ppermute | solution.py:12
  286.7 7.4 %bitcast_select_fusion.1 = f32[1280,1280]{0,1:T(8,128)} fusion(f32[1,1280,1280]{1,2,0:T(8,128)} %collective-permute-done, f32[768,768]{0,1:T(8,128)S(1)} %fusion.3, f32[768,512]{0,1:T(8,128)} %copy.12, f32[512,768]{0,1:T(8,128)} %bitcast.68, f32[512,512]{0,1:T(8,128)S(1)} %copy-done.4, pred[]{:T(512)S(6)} %eq.11), kind=kLoop, calls=%fused_computation.9 | loop fusion | flops 6553600 | bytes 19660800 | tf_op jit(solution)/shard_map/jit(_where)/select_n | solution.py:56
  294.1 8.2 %copy.13 = f32[1280,1280]{1,0:T(8,128)} copy(f32[1280,1280]{0,1:T(8,128)} %bitcast_select_fusion.1) | data formatting | bytes 13107200 | tf_op jit(solution)/shard_map/jit(_where)/select_n | solution.py:56
  302.3 8.2 %gather_fusion.2 = f32[768,1280]{1,0:T(8,128)} fusion(f32[1280,1280]{1,0:T(8,128)} %copy.13, s32[1024]{0:T(1024)S(1)} %pad_clamp_fusion.1), kind=kCustom, calls=%fused_computation.2.clone | custom fusion | bytes 7867392 | tf_op jit(solution)/shard_map/jit(_take)/gather | solution.py:18
  310.5 4.4 broadcast_select_fusion.1
  314.9 5.5 copy.14
  320.4 6.2 %gather_fusion.3 = f32[768,768]{1,0:T(8,128)} fusion(f32[768,1280]{0,1:T(8,128)} %copy.14, s32[1024]{0:T(1024)S(1)} %pad_clamp_fusion.1), kind=kCustom, calls=%fused_computation.4.clone | custom fusion | bytes 4721664 | tf_op jit(solution)/shard_map/jit(_take)/gather | solution.py:18
  326.6 2.0 fusion.2
  328.6 3.4 fusion.13
  332.0 3.2 fusion.27
  335.2 0.0 all-gather.14.cloned.1.call-start
  335.3 0.5 all-gather.14.cloned.1.call-update
  335.9 0.1 copy.26
  336.0 22.7 %reduce-scatter.6.cloned.1.call-done = f32[128,512]{0,1:T(8,128)} async-done(((f32[512,512]{0,1:T(8,128)}), f32[128,512]{0,1:T(8,128)}) %reduce-scatter.6.cloned.1.call-update) | async-done | bytes 262160 | tf_op jit(solution)/shard_map/reduce_scatter | solution.py:77
  358.7 1.7 bitcast_subtract_fusion.1
  360.5 0.0 reduce-scatter.8.cloned.1.call-start
  360.5 29.3 %all-gather.14.cloned.1.call-done = f32[768,512]{1,0:T(8,128)} async-done(((f32[192,512]{1,0:T(8,128)}), f32[768,512]{1,0:T(8,128)}) %all-gather.14.cloned.1.call-update) | async-done | bytes 1572880 | tf_op jit(solution)/shard_map/all_gather | solution.py:86
  389.8 3.0 copy.17
  392.8 28.2 %all-gather.12.cloned.1.call-done = f32[512,512]{0,1:T(8,128)} async-done(((f32[128,512]{0,1:T(8,128)}), f32[512,512]{0,1:T(8,128)}) %all-gather.12.cloned.1.call-update) | async-done | bytes 1048592 | tf_op jit(solution)/shard_map/all_gather | solution.py:85
  421.0 5.5 fusion
  427.2 0.6 fusion.37
  427.9 0.1 dynamic-slice.5
  428.0 75.4 %collective-permute-done.1 = f32[1,1280,1280]{1,2,0:T(8,128)} collective-permute-done((f32[1,1280,1280]{1,2,0:T(8,128)}, f32[1,1280,1280]{1,2,0:T(8,128)}, u32[]{:S(2)}, u32[]{:S(2)}) %collective-permute-start.1) | collective-permute-done | bytes 6553632 | tf_op jit(solution)/shard_map/ppermute | solution.py:12
  503.4 7.4 %bitcast_select_fusion = f32[1280,1280]{0,1:T(8,128)} fusion(f32[1,1280,1280]{1,2,0:T(8,128)} %collective-permute-done.1, f32[768,768]{0,1:T(8,128)S(1)} %fusion.2, f32[768,512]{0,1:T(8,128)} %copy.17, f32[512,768]{0,1:T(8,128)} %bitcast.70, f32[512,512]{0,1:T(8,128)S(1)} %copy-done.5, pred[]{:T(512)S(6)} %eq.12), kind=kLoop, calls=%fused_computation.8 | loop fusion | flops 6553600 | bytes 19660800 | tf_op jit(solution)/shard_map/jit(_where)/select_n | solution.py:56
  510.8 8.2 %copy.18 = f32[1280,1280]{1,0:T(8,128)} copy(f32[1280,1280]{0,1:T(8,128)} %bitcast_select_fusion) | data formatting | bytes 13107200 | tf_op jit(solution)/shard_map/jit(_where)/select_n | solution.py:56
  519.0 8.2 %gather_fusion.4 = f32[768,1280]{1,0:T(8,128)} fusion(f32[1280,1280]{1,0:T(8,128)} %copy.18, s32[1024]{0:T(1024)S(1)} %pad_clamp_fusion), kind=kCustom, calls=%fused_computation.3.clone | custom fusion | bytes 7867392 | tf_op jit(solution)/shard_map/jit(_take)/gather | solution.py:18
  527.2 4.4 broadcast_select_fusion
  531.6 5.5 copy.19
  537.1 5.6 gather_fusion.5
  542.6 0.2 select_bitcast_fusion
  542.9 3.5 fusion.16
  546.4 3.2 fusion.25
  549.6 0.1 copy.27
  549.8 1.1 pad_maximum_fusion
  550.9 22.3 %reduce-scatter.8.cloned.1.call-done = f32[128,512]{0,1:T(8,128)} async-done(((f32[512,512]{0,1:T(8,128)}), f32[128,512]{0,1:T(8,128)}) %reduce-scatter.8.cloned.1.call-update) | async-done | bytes 262160 | tf_op jit(solution)/shard_map/reduce_scatter | solution.py:77
  573.2 1.0 fusion.34
  574.2 0.1 pad_maximum_fusion.1
  574.3 1.1 copy.21
  (38 shorter events, 0.3 us)
Async XLA Ops:
  7.2 75.3 %all-gather.6.cloned.1.call-start = ((), (), s32[]{:S(2)}) async-start(), calls=%async_computation.3 | async-start | bytes 8192000 | tf_op jit(solution)/shard_map/all_gather | solution.py:38
  7.9 133.5 %reduce-scatter.4.cloned.1.call-start = ((), (), s32[]{:S(2)}) async-start(), calls=%async_computation.4 | async-start | bytes 1310720 | tf_op jit(solution)/shard_map/reduce_scatter | solution.py:77
  112.1 3.3 copy-start
  115.4 57.7 %all-gather.10.cloned.1.call-start = ((), (), s32[]{:S(2)}) async-start(), calls=%async_computation.6 | async-start | bytes 1966080 | tf_op jit(solution)/shard_map/all_gather | solution.py:86
  116.1 88.2 %all-gather.8.cloned.1.call-start = ((), (), s32[]{:S(2)}) async-start(), calls=%async_computation.5 | async-start | bytes 1310720 | tf_op jit(solution)/shard_map/all_gather | solution.py:85
  143.1 215.7 %reduce-scatter.6.cloned.1.call-start = ((), (), s32[]{:S(2)}) async-start(), calls=%async_computation.7 | async-start | bytes 1310720 | tf_op jit(solution)/shard_map/reduce_scatter | solution.py:77
  204.3 82.4 %copy-start.4 = (f32[512,512]{0,1:T(8,128)S(1)}, f32[512,512]{0,1:T(8,128)}, u32[]{:S(2)}) copy-start(f32[512,512]{0,1:T(8,128)} %all-gather.8.cloned.1.call-done) | copy-start | bytes 3145732
  209.8 76.8 %collective-permute-start = (f32[1,1280,1280]{1,2,0:T(8,128)}, f32[1,1280,1280]{1,2,0:T(8,128)}, u32[]{:S(2)}, u32[]{:S(2)}) collective-permute-start(f32[1,1280,1280]{1,2,0:T(8,128)} %fusion.1), channel_id=1, source_target_pairs={{0,4},{4,8},{8,12},{12,16},{16,20},{20,24},{24,28},{28,32},{32,36}... | collective-permute-start | bytes 19660808 | tf_op jit(solution)/shard_map/ppermute | solution.py:12
  328.6 7.3 %copy-start.9 = (f32[1,1,128,512]{3,2,1,0:T(8,128)S(1)}, f32[1,1,128,512]{3,2,1,0:T(8,128)}, u32[]{:S(2)}) copy-start(f32[1,1,128,512]{3,2,1,0:T(8,128)} %get-tuple-element.13) | copy-start | bytes 786436
  332.0 3.3 copy-start.2
  335.2 54.5 %all-gather.14.cloned.1.call-start = ((), (), s32[]{:S(2)}) async-start(), calls=%async_computation.9 | async-start | bytes 1966080 | tf_op jit(solution)/shard_map/all_gather | solution.py:86
  335.8 85.2 %all-gather.12.cloned.1.call-start = ((), (), s32[]{:S(2)}) async-start(), calls=%async_computation.8 | async-start | bytes 1310720 | tf_op jit(solution)/shard_map/all_gather | solution.py:85
  360.5 212.7 %reduce-scatter.8.cloned.1.call-start = ((), (), s32[]{:S(2)}) async-start(), calls=%async_computation.10 | async-start | bytes 1310720 | tf_op jit(solution)/shard_map/reduce_scatter | solution.py:77
  421.0 82.4 %copy-start.5 = (f32[512,512]{0,1:T(8,128)S(1)}, f32[512,512]{0,1:T(8,128)}, u32[]{:S(2)}) copy-start(f32[512,512]{0,1:T(8,128)} %all-gather.12.cloned.1.call-done) | copy-start | bytes 3145732
  426.5 76.8 %collective-permute-start.1 = (f32[1,1280,1280]{1,2,0:T(8,128)}, f32[1,1280,1280]{1,2,0:T(8,128)}, u32[]{:S(2)}, u32[]{:S(2)}) collective-permute-start(f32[1,1280,1280]{1,2,0:T(8,128)} %fusion), channel_id=1, source_target_pairs={{0,4},{4,8},{8,12},{12,16},{16,20},{20,24},{24,28},{28,32},{32,36}... | collective-permute-start | bytes 19660808 | tf_op jit(solution)/shard_map/ppermute | solution.py:12
  542.9 6.7 %copy-start.8 = (f32[1,1,128,512]{3,2,1,0:T(8,128)S(1)}, f32[1,1,128,512]{3,2,1,0:T(8,128)}, u32[]{:S(2)}) copy-start(f32[1,1,128,512]{3,2,1,0:T(8,128)} %get-tuple-element.12) | copy-start | bytes 786436
  542.9 6.9 %copy-start.1 = (f32[192,512]{1,0:T(8,128)S(1)}, f32[192,512]{1,0:T(8,128)}, u32[]{:S(2)}) copy-start(f32[192,512]{1,0:T(8,128)} %copy-done) | copy-start | bytes 1179652
  542.9 6.9 %copy-start.3 = (f32[192,512]{1,0:T(8,128)S(1)}, f32[192,512]{1,0:T(8,128)}, u32[]{:S(2)}) copy-start(f32[192,512]{1,0:T(8,128)} %copy-done.2) | copy-start | bytes 1179652
  546.4 27.8 %copy-start.6 = (f32[128,512]{0,1:T(8,128)S(1)}, f32[128,512]{0,1:T(8,128)}, u32[]{:S(2)}) copy-start(f32[128,512]{0,1:T(8,128)} %bitcast_subtract_fusion.2) | copy-start | bytes 786436
  546.4 27.8 %copy-start.7 = (f32[128,512]{0,1:T(8,128)S(1)}, f32[128,512]{0,1:T(8,128)}, u32[]{:S(2)}) copy-start(f32[128,512]{0,1:T(8,128)} %bitcast_subtract_fusion.1) | copy-start | bytes 786436
Sparse Core Ops, SparseCore 0:
  9.8 72.6 all-gather.5
  115.5 25.8 reduce-scatter.3
  143.9 29.1 all-gather.9
  174.9 29.4 all-gather.7
  335.3 23.3 reduce-scatter.5
  360.4 29.3 all-gather.13
  391.6 29.4 all-gather.11
  549.7 23.4 reduce-scatter.7
where the time goes:
time: 585 us; the launch traced here: 582 us
  waiting for transfers between devices  404 us (69%)
  local copies, waits for them, and re-layouts  91.7 us (16%)
  other arithmetic  50.8 us (9%)
  matrix products  19.8 us (3%)
  between operations  15.8 us (3%)
    ppermute x2, waiting for transfers between devices, from_behind(): return lax.ppermute(value, axis, pairs)  151 us
    reduce_scatter x3, waiting for transfers between devices, local(): lax.psum_scatter(partial_term(jnp.int32(0), lax.axis_size('panel') * narr...  68.2 us
    all_gather x1, waiting for transfers between devices, local(): top_full = lax.all_gather(top_inverse, 'panel', axis=0, tiled=True)  67 us
    all_gather x2, waiting for transfers between devices, local(): lax.all_gather(off_rows, 'panel', axis=0, tiled=True)  59.2 us
    all_gather x2, waiting for transfers between devices, local(): lax.all_gather(diag_rows, 'panel', axis=0, tiled=True)  56.5 us
    gather x3, local copies, waits for them, and re-layouts, extract_block(): jnp.take(parent_block, row_index, axis=0)  24.5 us
    gather x3, local copies, waits for them, and re-layouts, extract_block(): jnp.take(jnp.take(parent_block, row_index, axis=0), row_index, axis=1)  18 us
    select_n x3, local copies, waits for them, and re-layouts, extract_block(): jnp.take(parent_block, row_index, axis=0)  16.5 us
  transfers between devices with their start and end apart: 10, of which 10 were waited for; matrix products, arithmetic and copies ran while one was open for 4% of the time, Pallas kernels for 0%

commit v1 on v0

v1 whole, which is shorter than its diff:
```python
import functools

import jax
import jax.numpy as jnp
from jax import lax
from jax.experimental import pallas as pl
from jax.experimental.pallas import tpu as pltpu
from jax.sharding import PartitionSpec as P

F32 = jnp.float32
BF16 = jnp.bfloat16
MESH = pl.DeviceIdType.MESH

T = 1280
B = 512
SR = 768
J0 = T
J1 = T + B
N2 = T + 2 * B
SHARD = T // 4
HALF = SHARD // 2
SUB = HALF // 2
RQ = SR // 4
BQ = B // 4


def split(x):
    hi = x.astype(BF16)
    return hi, (x - hi.astype(F32)).astype(BF16)


def mm(a, b):
    return jnp.dot(a, b, preferred_element_type=F32)


def mm3(a, bh, bl):
    ah, al = split(a)
    return mm(ah, bh) + (mm(ah, bl) + mm(al, bh))


def mmf(a, b):
    bh, bl = split(b)
    return mm3(a, bh, bl)


def one_hot(g, base, rows):
    at = lax.broadcasted_iota(jnp.int32, (rows, SR), 0) + base
    return jnp.where(at == g, 1.0, 0.0).astype(BF16)


def compose(h, pos):
    column = jnp.broadcast_to(h.astype(F32), (128, SR)).T
    at = lax.broadcasted_iota(jnp.int32, (SR, 128), 0)
    parts = []
    for block in range(SR // 128):
        hit = at == pos[:, 128 * block:128 * (block + 1)]
        parts.append(jnp.sum(jnp.where(hit, column, 0.0), axis=0, keepdims=True))
    return jnp.concatenate(parts, axis=1).astype(jnp.int32)


def kernel(
    top, dinv, ufac, pm, ln, rm,
    diag_out, off_out,
    z, u0, u0r, u1, u2, uh, ul, v0h, v0l, v1h, v1l, s0, s2, s2c, gat,
    d0w, d0r, d0, d1, dq2, inn_send, inn_recv, oc, gv, gt, gs,
    lsem, ysend, yrecv, ssend, srecv, hsend, hrecv, gsend, grecv, asend, arecv, isend, irecv,
):
    n = lax.axis_index("snode")
    k = lax.axis_index("panel")
    count = lax.axis_size("snode")
    nxt = lax.rem(n + 1, count)
    prv = lax.rem(n + count - 1, count)
    core = lax.rem(n, 2)
    sib = n + 1 - 2 * core
    right, left, opp = lax.rem(k + 1, 4), lax.rem(k + 3, 4), lax.rem(k + 2, 4)
    around = (right, opp, left)

    barrier = pltpu.get_barrier_semaphore()
    for who in ({"panel": left}, {"panel": right}, {"panel": opp}, {"snode": sib}, {"snode": prv}):
        pl.semaphore_signal(barrier, inc=1, device_id=who, device_id_type=MESH)

    def rows(start, size):
        return pl.ds(pl.multiple_of(start, 8), size)

    def local_copy(src, dst, at):
        return pltpu.make_async_copy(src, dst, lsem.at[at])

    def remote(src, dst, ss, rs, who):
        return pltpu.make_async_remote_copy(
            src_ref=src, dst_ref=dst, send_sem=ss, recv_sem=rs, device_id=who, device_id_type=MESH
        )

    loads = [
        local_copy(top, z.at[rows(SHARD * k, SHARD), pl.ds(0, T)], 0),
        local_copy(ufac.at[1, 0], u1, 1),
        local_copy(ufac.at[0, 0], u0, 2),
        local_copy(dinv.at[0, 0], d0w, 3),
        local_copy(ufac.at[2, 0], u2, 4),
        local_copy(dinv.at[1, 0], d1.at[rows(BQ * k, BQ)], 5),
        local_copy(dinv.at[2, 0], dq2, 6),
    ]
    for copy in loads:
        copy.start()
    pl.semaphore_wait(barrier, 5)

    sends = []

    def send(src, dst, ss, rs, who):
        copy = remote(src, dst, ss, rs, who)
        copy.start()
        sends.append(copy)

    def arrived(dst, rs):
        remote(dst, dst, rs, rs, {"panel": right}).wait_recv()

    def piece(shard, c, part):
        return z.at[rows(SHARD * shard + HALF * c + SUB * part, SUB), pl.ds(0, T)]

    def own(part):
        return top.at[rows(HALF * core + SUB * part, SUB), :]

    to_r, to_l = {"panel": right}, {"panel": left}
    send(own(0), piece(k, core, 0), ysend.at[0], yrecv.at[0], to_r)
    send(own(1), piece(k, core, 1), ysend.at[1], yrecv.at[1], to_l)
    send(ufac.at[0, 0], u0r, hsend.at[0], hrecv.at[0], {"snode": nxt})
    send(dinv.at[0, 0], d0r, hsend.at[1], hrecv.at[1], {"snode": nxt})
    send(own(1), piece(k, core, 1), ysend.at[2], yrecv.at[2], to_r)
    send(own(0), piece(k, core, 0), ysend.at[3], yrecv.at[3], to_l)

    def service(at):
        shard, part = ((left, 0), (right, 1), (left, 1), (right, 0), (opp, 0), (opp, 1))[at]
        here = piece(shard, core, part)
        arrived(here, yrecv.at[at])
        if at == 0:
            send(here, here, ysend.at[4], yrecv.at[4], to_r)
        if at == 1:
            send(here, here, ysend.at[5], yrecv.at[5], to_l)
        send(here, here, ssend.at[at], srecv.at[at], {"snode": sib})

    def service_sib(at):
        shard, part = ((left, 0), (right, 1), (left, 1), (right, 0), (opp, 0), (opp, 1))[at]
        arrived(piece(shard, 1 - core, part), srecv.at[at])

    p0 = pm[0, n]
    p1 = pm[1, n]
    lane = lax.broadcasted_iota(jnp.int32, (1, SR), 1)
    h0 = jnp.where(lane < ln[0, p0], rm[pl.ds(p0, 1), :], -1)
    g0 = jnp.where(lane < ln[0, n], rm[pl.ds(n, 1), :], -1)
    r1 = rm[pl.ds(count + n, 1), :]
    g1 = jnp.where(r1 < B, r1 + J0, compose(h0, r1 - B))
    g1 = jnp.where(lane < ln[1, n], g1, -1)
    r2 = rm[pl.ds(2 * count + n, 1), :]
    g2 = jnp.where(lane < ln[2, n], jnp.where(r2 < B, r2 + J1, compose(g1, r2 - B)), -1)
    r2c = rm[pl.ds(2 * count + nxt, 1), :]
    g2c = jnp.where(lane < ln[2, nxt], jnp.where(r2c < B, r2c + J1, compose(g1, r2c - B)), -1)
    lists = jnp.concatenate([g0, g1, g2, g2c, g0, g1, g2, g2c], axis=0)
    gv[...] = jnp.maximum(lists, 0)
    gt[...] = jnp.concatenate([lists.astype(F32)] * 16, axis=0).T
    to_smem = local_copy(gv, gs, 7)
    to_smem.start()

    def scatter(g, vh, vl, tiles):
        @pl.loop(0, tiles)
        def _(i):
            s = one_hot(g, 256 * i, 256)
            here = rows(256 * i, 256)
            vh[here, :] = mm(s, uh[...]).astype(BF16)
            vl[here, :] = mm(s, ul[...]).astype(BF16)

    def load_u(value):
        uh[...], ul[...] = split(value)

    loads[1].wait()
    load_u(u1[...])
    scatter(g1, v1h, v1l, J1 // 256)

    def build(g, s, tiles):
        @pl.loop(0, tiles)
        def _(i):
            s[rows(256 * i, 256), :] = one_hot(g, 256 * i, 256)

    service(0)
    service(1)
    build(g0, s0, T // 256)
    build(g2c, s2c, N2 // 256)
    build(g2, s2, N2 // 256)

    def stream1(shard):
        here = rows(SHARD * shard, SHARD)
        t = z[here, 0:T]
        z[here, J1:N2] = -mm3(t, v1h[0:T, :], v1l[0:T, :])

    def stream0(shard):
        here = rows(SHARD * shard, SHARD)
        t = z[here, 0:T]
        z[here, J0:J1] = -mm3(t, v0h[...], v0l[...])

    loads[0].wait()
    stream1(k)
    service(2)
    service(3)

    for at in (2, 3):
        loads[at].wait()
    arrived(d0r, hrecv.at[1])
    mine0 = p0 == n
    d0_here = rows(BQ * k, BQ)
    d0[d0_here, :] = jnp.where(mine0, d0w[...], d0r[...])

    def gather_d(ref, at):
        for hop in range(3):
            send(ref.at[d0_here], ref.at[d0_here], gsend.at[at, hop], grecv.at[at, hop], {"panel": around[hop]})

    def gathered_d(ref, at):
        for hop in range(3):
            arrived(ref.at[rows(BQ * lax.rem(k + 3 - hop, 4), BQ)], grecv.at[at, hop])

    gather_d(d0, 0)
    loads[5].wait()
    gather_d(d1, 1)

    arrived(u0r, hrecv.at[0])
    load_u(jnp.where(mine0, u0[...], u0r[...]))
    scatter(h0, v0h, v0l, T // 256)
    stream0(k)
    service_sib(0)
    service_sib(1)
    service_sib(2)
    service_sib(3)
    stream1(left)
    stream0(left)
    service(4)
    service(5)
    stream1(right)
    stream0(right)
    service_sib(4)
    service_sib(5)
    stream1(opp)
    stream0(opp)

    to_smem.wait()

    def live(row):
        return gt[rows(RQ * k, RQ), row:row + 1] >= 0.0

    def extract(row, kdim, s):
        @pl.loop(0, RQ, unroll=8)
        def _(a):
            gat[pl.ds(a, 1), 0:kdim] = z[pl.ds(gs[row, RQ * k + a], 1), 0:kdim]

        gh, gl = split(gat[:, 0:kdim])
        inner = mm(gh, s[...]) + mm(gl, s[...])
        return jnp.where(live(row), inner, 0.0)

    def finish_off(level, slot, inner, u):
        uh[...], ul[...] = split(u[...])
        off_out[level, 0] = -mm3(inner, uh[...], ul[...])
        for hop in range(3):
            j = around[hop]
            send(
                off_out.at[level, 0, :, pl.ds(pl.multiple_of(BQ * j, BQ), BQ)],
                oc.at[slot, rows(RQ * k, RQ)],
                asend.at[slot, hop], arecv.at[slot, hop], {"panel": j},
            )
        keep = pltpu.make_async_copy(
            off_out.at[level, 0, :, pl.ds(pl.multiple_of(BQ * k, BQ), BQ)],
            oc.at[slot, rows(RQ * k, RQ)], lsem.at[8 + slot],
        )
        keep.start()
        return keep

    def finish_diag(level, slot, keep, d, u):
        for hop in range(3):
            arrived(oc.at[slot, rows(RQ * lax.rem(k + 3 - hop, 4), RQ)], arecv.at[slot, hop])
        keep.wait()
        diag_out[level, 0] = d - mmf(oc[slot].T, u[...])

    keep0 = finish_off(0, 0, extract(0, T, s0), u0)

    z[J0:J1, 0:T] = z[0:T, J0:J1].T
    gathered_d(d0, 0)
    z[J0:J1, J0:J1] = d0[...] - mm3(z[J0:J1, 0:T], v0h[...], v0l[...])
    z[J0:J1, J1:N2] = -mm3(z[J0:J1, 0:J1], v1h[...], v1l[...])

    @pl.loop(0, 4)
    def _(i):
        here = rows(SHARD * i, SHARD)
        z[here, J1:N2] = z[here, J1:N2] - mm3(z[here, J0:J1], v1h[J0:J1, :], v1l[J0:J1, :])

    z[J1:N2, 0:J1] = z[0:J1, J1:N2].T
    gathered_d(d1, 1)
    z[J1:N2, J1:N2] = d1[...] - mm3(z[J1:N2, 0:J1], v1h[...], v1l[...])

    inn_send[...] = extract(3, N2, s2c)
    send(inn_send, inn_recv, isend.at[0], irecv.at[0], {"snode": nxt})
    inner_mine = extract(2, N2, s2)
    finish_diag(0, 0, keep0, d0w[...], u0)

    @pl.loop(0, RQ, unroll=8)
    def _(a):
        off_out[1, 0, pl.ds(a, 1), :] = z[pl.ds(gs[1, RQ * k + a], 1), J1:N2]

    off_out[1, 0] = jnp.where(live(1), off_out[1, 0], 0.0)
    diag_out[1, 0] = z[rows(J1 + BQ * k, BQ), J1:N2]

    loads[4].wait()
    loads[6].wait()
    arrived(inn_recv, irecv.at[0])
    inner2 = jnp.where(p1 == n, inner_mine, inn_recv[...])
    keep2 = finish_off(2, 1, inner2, u2)
    finish_diag(2, 1, keep2, dq2[...], u2)

    for copy in sends:
        copy.wait_send()


def local(top_inverse, diag_inverse, u_factor, parent_map, lengths, rows_map):
    dma = pltpu.SemaphoreType.DMA
    vm, hbm, sm = (pl.BlockSpec(memory_space=m) for m in (pltpu.VMEM, pl.ANY, pltpu.SMEM))
    return pl.pallas_call(
        kernel,
        out_shape=(
            jax.ShapeDtypeStruct((3, 1, BQ, B), F32),
            jax.ShapeDtypeStruct((3, 1, RQ, B), F32),
        ),
        in_specs=[hbm, hbm, hbm, sm, sm, vm],
        out_specs=(vm, vm),
        scratch_shapes=[
            pltpu.VMEM((N2, N2), F32),
            pltpu.VMEM((SR, B), F32),
            pltpu.VMEM((SR, B), F32),
            pltpu.VMEM((SR, B), F32),
            pltpu.VMEM((SR, B), F32),
            pltpu.VMEM((SR, B), BF16),
            pltpu.VMEM((SR, B), BF16),
            pltpu.VMEM((T, B), BF16),
            pltpu.VMEM((T, B), BF16),
            pltpu.VMEM((J1, B), BF16),
            pltpu.VMEM((J1, B), BF16),
            pltpu.VMEM((T, SR), BF16),
            pltpu.VMEM((N2, SR), BF16),
            pltpu.VMEM((N2, SR), BF16),
            pltpu.VMEM((RQ, N2), F32),
            pltpu.VMEM((BQ, B), F32),
            pltpu.VMEM((BQ, B), F32),
            pltpu.VMEM((B, B), F32),
            pltpu.VMEM((B, B), F32),
            pltpu.VMEM((BQ, B), F32),
            pltpu.VMEM((RQ, SR), F32),
            pltpu.VMEM((RQ, SR), F32),
            pltpu.VMEM((2, SR, BQ), F32),
            pltpu.VMEM((8, SR), jnp.int32),
            pltpu.VMEM((SR, 128), F32),
            pltpu.SMEM((8, SR), jnp.int32),
            dma((10,)), dma((6,)), dma((6,)), dma((6,)), dma((6,)),
            dma((2,)), dma((2,)), dma((2, 3)), dma((2, 3)), dma((2, 3)), dma((2, 3)),
            dma((1,)), dma((1,)),
        ],
        compiler_params=pltpu.CompilerParams(
            collective_id=0, has_side_effects=True, vmem_limit_bytes=62 * 1024 * 1024
        ),
    )(
        top_inverse, diag_inverse, u_factor, parent_map, lengths,
        rows_map.reshape(3 * rows_map.shape[1], SR),
    )


def solution(mesh):
    return jax.shard_map(
        local,
        mesh=mesh,
        in_specs=(
            P("panel", None),
            P(None, "snode", "panel", None),
            P(None, "snode", None, None),
            P(),
            P(),
            P(),
        ),
        out_specs=(P(None, "snode", "panel", None), P(None, "snode", "panel", None)),
        check_vma=False,
    )
```

time: 585 us -> 89.5 us (0.15)
  waiting for transfers between devices: 404 us -> 0 us
  local copies, waits for them, and re-layouts: 91.7 us -> 3.18 us
  Pallas kernels: 0 us -> 85.5 us
  other arithmetic: 50.8 us -> 0 us
  matrix products: 19.8 us -> 0 us
  between operations: 15.8 us -> 0.65 us
    all_gather x5 -> x0, waiting for transfers between devices: 183 us -> none  [the longest x1 67 us: local(): top_full = lax.all_gather(top_inverse, 'panel', axis=0, tiled=True)]
    ppermute x2 -> x0, waiting for transfers between devices: 151 us -> none  [from_behind(): return lax.ppermute(value, axis, pairs)]
    pallas_call x0 -> x1, Pallas kernels: none -> 85.5 us  [local(): pl.pallas_call(kernel, out_shape=(jax.ShapeDtypeStruct((3, 1, BQ, B), F32...]
    reduce_scatter x3 -> x0, waiting for transfers between devices: 68.2 us -> none  [local(): lax.psum_scatter(partial_term(jnp.int32(0), lax.axis_size('panel') * narr...]
    gather x6 -> x0, local copies, waits for them, and re-layouts: 42.4 us -> none  [the longest x3 24.5 us: extract_block(): jnp.take(parent_block, row_index, axis=0)]
    select_n x5 -> x0, local copies, waits for them, and re-layouts: 32.8 us -> none  [the longest x3 16.5 us: extract_block(): jnp.take(parent_block, row_index, axis=0)]
    select_n x9 -> x0, other arithmetic: 28.4 us -> none  [the longest x2 14.9 us: local(): jnp.where(parent // slot_count == owner_index, stacked[parent % slot_coun...]
    dot_general x6 -> x0, matrix products: 19.8 us -> none  [the longest x3 10.2 us: local(): off_rows = -jnp.dot(inner_rows, u_block, precision=HIGHEST)]
  transfers between devices with their start and end apart: 10 -> 0, of which waited for: 10 -> 0; matrix products, arithmetic and copies ran while one was open for 4% -> 0% of each run, Pallas kernels for 0% -> 0%
where the time goes in v1:
time: 89.5 us; the launch traced here: 89.3 us
  Pallas kernels  85.5 us (96%)
  local copies, waits for them, and re-layouts  3.18 us (4%)
    pallas_call x1, Pallas kernels, local(): pl.pallas_call(kernel, out_shape=(jax.ShapeDtypeStruct((3, 1, BQ, B), F32...  85.5 us
    unnamed x4, local copies, waits for them, and re-layouts  3.18 us

profile of v1, /device:TPU:16, one launch (start us, length us, event | category | flops | bytes accessed | tf_op | source)
XLA Modules:
  0.0 89.3 jit_solution(2040091388018878537)
XLA Ops:
  0.6 85.5 %shard_map.77 = (f32[3,1,128,512]{3,2,1,0:T(8,128)}, f32[3,1,192,512]{3,2,1,0:T(8,128)}) custom-call(f32[320,1280]{1,0:T(8,128)} %top.1, f32[3,1,128,512]{3,2,1,0:T(8,128)} %dinv.1, f32[3,1,768,512]{3,2,1,0:T(8,128)} %ufac.1, s32[2,64]{1,0:T(2,128)} %pm.1, s32[3,64]{1,0:T(4,128)} %ln.1, s32[192,768]{1,0:T(8,128)} %bitcast.1), custom_call_target="tpu_custom_call" | custom-call | tf_op jit(solution)/shard_map/pallas_call | solution.py:320
  86.2 0.0 copy-start
  86.2 2.2 %copy.10 = f32[3,1,128,512]{3,2,1,0:T(8,128)} copy(f32[3,1,128,512]{3,2,1,0:T(8,128)} %get-tuple-element.4) | data formatting | bytes 1572864
  88.3 0.0 copy-done
  88.3 1.0 %copy.11 = f32[3,1,192,512]{3,2,1,0:T(8,128)} copy(f32[3,1,192,512]{3,2,1,0:T(8,128)S(1)} %copy-done) | data formatting | bytes 2359296
Async XLA Ops:
  86.2 2.2 %copy-start = (f32[3,1,192,512]{3,2,1,0:T(8,128)S(1)}, f32[3,1,192,512]{3,2,1,0:T(8,128)}, u32[]{:S(2)}) copy-start(f32[3,1,192,512]{3,2,1,0:T(8,128)} %get-tuple-element.5) | copy-start | bytes 3538948
